TPU v7x, 32 devices: a whole 2x2x4 slice. The times are simulated.
32 devices in a mesh: section: 2 (over x), ctx: 16 (over z, y, core).
Axes of the slice: x: 2, y: 2, z: 4, core: 2. Of those that a mesh axis runs over, the one named last changes fastest.
Arguments:
- doc_lengths: int32 [7], replicated, may hold values from 1 to 1152, 4096 in all
- queries: bfloat16 [4096, 8192], P('ctx', 'section'), may hold values from -6 to 6
- key_states: bfloat16 [4096, 1024], P('ctx', 'section'), may hold values from -6 to 6
- value_states: bfloat16 [4096, 1024], P('ctx', 'section'), may hold values from -6 to 6
Outputs:
- attended: bfloat16 [4096, 8192], P(('ctx', 'section'))
Inputs may be any that keep to these rules, and one draw needn't show every extreme that they name: `doc_lengths`: they sum to 4096; the longest is exactly 1152.
All inputs are finite; a program needn't handle non-finite values.
Results may differ from a plain program's by a relative error of at most 0.0037.
Values may be sent and summed in bfloat16 or wider, within the bound.
A program may use at most 64 MiB of HBM per device.

v0:
```python
import functools
import math

import jax
import jax.numpy as jnp
from jax import lax
from jax.experimental import pallas as pl
from jax.experimental.pallas import tpu as pltpu
from jax.sharding import PartitionSpec as P

Q_HEADS = 64
KV_HEADS = 8
HEAD = 128
MOST = 1152
GROUP = Q_HEADS // KV_HEADS
BLOCK = 128
MESH = pl.DeviceIdType.MESH
SCALE = math.log2(math.e) / math.sqrt(HEAD)
UP, SIDE, SIB_A, SIB_B, SIB_C, HALF_Y, HALF_Z = range(7)


def kernel(n_sec, n_ctx, docs_ref, q_ref, k_ref, v_ref, out_ref, kv, q, obuf, bias,
           in_sem, q_sem, send_sem, recv_sem, osend_sem, orecv_sem, own_sem):
    heads = kv.shape[0]
    tokens = q.shape[0]
    span = MOST + BLOCK
    rows_out = tokens // n_sec
    per_block = BLOCK // rows_out
    width = GROUP * HEAD
    sec = lax.axis_index("section")
    me = lax.axis_index("ctx")
    j = lax.rem(me, 2)
    pair = lax.div(me, 2)
    y = lax.rem(pair, 2)
    z = lax.div(pair, 2)
    n_z = n_ctx // 4
    low = 3 * 2 * tokens - MOST

    def rows(slot):
        return pl.ds(pl.multiple_of(slot * tokens - low, BLOCK), tokens)

    def half(start):
        return pl.ds(start, BLOCK)

    has_down = z > 0
    has_up = z < n_z - 1
    has_c = pair > 0
    is_giver = (y == 0) & (j == 1)

    half_y_src = half(3 * tokens - low + BLOCK)
    half_z_src = half(5 * tokens - low + BLOCK)

    def send(kind, h):
        src, dst, to = {
            UP: lambda: (rows(6 + j), rows(2 + j), me + 4),
            SIDE: lambda: (rows(6 + j - 4 * y), rows(4 + j), me + 2 - 4 * y),
            SIB_A: lambda: (rows(6), rows(6), me + 1),
            SIB_B: lambda: (rows(2 + j), rows(2 + j), me + 1 - 2 * j),
            SIB_C: lambda: (rows(4 + j), rows(4 + j), me + 1 - 2 * j),
            HALF_Y: lambda: (half_y_src, half(0), me + 1),
            HALF_Z: lambda: (half_z_src, half(0), me + 3),
        }[kind]()
        return pltpu.make_async_remote_copy(
            src_ref=kv.at[h, src], dst_ref=kv.at[h, dst],
            send_sem=send_sem.at[kind, h], recv_sem=recv_sem.at[kind, h],
            device_id={"ctx": to}, device_id_type=MESH)

    def wait_recv(kind, h):
        dst = {
            UP: lambda: rows(2 + j),
            SIDE: lambda: rows(4 + j),
            SIB_A: lambda: rows(6),
            SIB_B: lambda: rows(3 - j),
            SIB_C: lambda: rows(5 - j),
            HALF_Y: lambda: half(0),
            HALF_Z: lambda: half(0),
        }[kind]()
        pltpu.make_async_remote_copy(
            src_ref=kv.at[h, dst], dst_ref=kv.at[h, dst],
            send_sem=send_sem.at[kind, h], recv_sem=recv_sem.at[kind, h],
            device_id={"ctx": me}, device_id_type=MESH).wait_recv()

    def load(h, which):
        ref = (k_ref, v_ref)[which]
        return pltpu.make_async_copy(
            ref.at[:, pl.ds(h * HEAD, HEAD)],
            kv.at[h, rows(6 + j), pl.ds(which * HEAD, HEAD)], in_sem.at[which, h])

    def load_q():
        return pltpu.make_async_copy(q_ref, q, q_sem)

    for h in range(heads):
        load(h, 0).start()
        load(h, 1).start()
    load_q().start()

    barrier = pltpu.get_barrier_semaphore()
    greets = [(None, {"ctx": me + 1 - 2 * j}), (None, {"ctx": me + 2 - 4 * y}),
              (has_up, {"ctx": me + 4}), (has_down, {"ctx": me - 4}),
              (is_giver, {"ctx": me + 1}), ((y == 1) & (j == 0), {"ctx": me - 1}),
              (is_giver & has_up, {"ctx": me + 3}),
              ((y == 0) & (j == 0) & has_down, {"ctx": me - 3})]
    greets += [(None, {"section": lax.rem(sec + step, n_sec)}) for step in range(1, n_sec)]

    def when(condition, action):
        if condition is None:
            action()
        else:
            pl.when(condition)(action)

    for condition, to in greets:
        when(condition, functools.partial(
            pl.semaphore_signal, barrier, inc=1, device_id=to, device_id_type=MESH))
    peers = sum(1 if condition is None else jnp.where(condition, 1, 0)
                for condition, _ in greets)
    pl.semaphore_wait(barrier, peers)

    for h in range(heads):
        load(h, 0).wait()
        load(h, 1).wait()
        when(has_up, lambda: send(UP, h).start())
        when(y == 0, lambda: send(SIDE, h).start())
        when(j == 0, lambda: send(SIB_A, h).start())

    def clear(first, count):
        kv[:, first:first + count, :] = jnp.zeros((heads, count, 2 * HEAD), kv.dtype)

    when(z == 0, lambda: clear(2 * tokens - low, 2 * tokens))
    when(pair == 0, lambda: clear(4 * tokens - low, 2 * tokens))
    when((j == 0) & (pair < 3), lambda: clear(0, BLOCK))

    for b in range(tokens // BLOCK):
        first = me * tokens + b * BLOCK
        pos = first + lax.broadcasted_iota(jnp.int32, (BLOCK, 1), 0)
        start = jnp.zeros((BLOCK, 1), jnp.int32)
        end = jnp.int32(0)
        for d in range(docs_ref.shape[0]):
            end = end + docs_ref[d]
            start = jnp.where(pos >= end, end, start)
        key = first - MOST + lax.broadcasted_iota(jnp.int32, (BLOCK, span), 1)
        bias[b] = jnp.where((key >= start) & (key <= pos), 0.0, -1e30)

    def forward(h):
        @pl.when(has_down)
        def _():
            wait_recv(UP, h)
            when(y == 1, lambda: send(SIDE, h).start())
            send(SIB_B, h).start()
            when(is_giver, lambda: send(HALF_Y, h).start())

        @pl.when(has_c)
        def _():
            wait_recv(SIDE, h)
            send(SIB_C, h).start()
            when(is_giver & has_up, lambda: send(HALF_Z, h).start())

    def arrive(h):
        when(j == 1, lambda: wait_recv(SIB_A, h))
        when(has_down, lambda: wait_recv(SIB_B, h))
        when(has_c, lambda: wait_recv(SIB_C, h))
        when((y == 1) & (j == 0) & has_down, lambda: wait_recv(HALF_Y, h))
        when((y == 0) & (j == 0) & (z > 1), lambda: wait_recv(HALF_Z, h))

    def out_columns(source, h):
        return pl.ds(pl.multiple_of((source * heads + h) * width, width), width)

    def give(h, dest):
        piece = pl.ds(pl.multiple_of(dest * rows_out, rows_out), rows_out)
        return pltpu.make_async_remote_copy(
            src_ref=obuf.at[h, piece], dst_ref=out_ref.at[:, out_columns(sec, h)],
            send_sem=osend_sem.at[h, dest], recv_sem=orecv_sem.at[h, sec],
            device_id={"section": dest}, device_id_type=MESH)

    def take(h, source):
        piece = pl.ds(pl.multiple_of(source * rows_out, rows_out), rows_out)
        return pltpu.make_async_remote_copy(
            src_ref=obuf.at[h, piece], dst_ref=out_ref.at[:, out_columns(source, h)],
            send_sem=osend_sem.at[h, source], recv_sem=orecv_sem.at[h, source],
            device_id={"section": source}, device_id_type=MESH)

    def keep(h):
        piece = pl.ds(pl.multiple_of(sec * rows_out, rows_out), rows_out)
        return pltpu.make_async_copy(
            obuf.at[h, piece], out_ref.at[:, out_columns(sec, h)], own_sem.at[h])

    def unit(h, b):
        window = pl.ds(pl.multiple_of(j * tokens + b * BLOCK, BLOCK), span)
        lines = pl.ds(pl.multiple_of(b * BLOCK, BLOCK), BLOCK)
        keys = kv[h, window, 0:HEAD]
        values = jnp.concatenate(
            [kv[h, window, HEAD:2 * HEAD], jnp.ones((span, HEAD), kv.dtype)], 1)
        mask = bias[b]
        part = 4
        for first in range(0, GROUP, part):
            columns = pl.ds(pl.multiple_of(h * width + first * HEAD, HEAD), part * HEAD)
            wide = q[lines, columns]
            rows_q = jnp.concatenate(
                [wide[:, i * HEAD:(i + 1) * HEAD] for i in range(part)], 0)
            scores = lax.dot_general(rows_q, keys, (((1,), (1,)), ((), ())),
                                     preferred_element_type=jnp.float32)
            scores = (scores.reshape(part, BLOCK, span) + mask[None]).reshape(
                part * BLOCK, span)
            top = jnp.max(scores, axis=1, keepdims=True)
            weights = jnp.exp2((scores - top) * SCALE).astype(jnp.bfloat16)
            mixed = jnp.dot(weights, values, preferred_element_type=jnp.float32)
            result = (mixed[:, :HEAD] / mixed[:, HEAD:]).astype(obuf.dtype)
            for i in range(part):
                at = (first + i) * HEAD
                obuf[h, lines, at:at + HEAD] = result[i * BLOCK:(i + 1) * BLOCK]

    blocks = tokens // BLOCK
    my_block = lax.div(sec * rows_out, BLOCK)
    forward(0)
    load_q().wait()

    def step(t, carry):
        h = lax.div(t, blocks)
        turn = lax.rem(t, blocks)
        b = lax.rem(my_block + 1 + turn, blocks)

        when(turn == 0, lambda: arrive(h))
        when((turn == 1) & (h + 1 < heads), lambda: forward(h + 1))
        unit(h, b)
        for i in range(per_block):
            dest = b * per_block + i
            when(dest != sec, lambda: give(h, dest).start())
            when(dest == sec, lambda: keep(h).start())
        return carry

    lax.fori_loop(0, heads * blocks, step, 0)

    def finish(h, carry):
        when(has_up, lambda: send(UP, h).wait_send())
        when((y == 0) | has_down, lambda: send(SIDE, h).wait_send())
        when(j == 0, lambda: send(SIB_A, h).wait_send())
        when(has_down, lambda: send(SIB_B, h).wait_send())
        when(has_c, lambda: send(SIB_C, h).wait_send())
        when(is_giver & has_down, lambda: send(HALF_Y, h).wait_send())
        when(is_giver & has_down & has_up, lambda: send(HALF_Z, h).wait_send())
        keep(h).wait()
        for offset in range(1, n_sec):
            other = lax.rem(sec + offset, n_sec)
            give(h, other).wait_send()
            take(h, other).wait_recv()
        return carry

    lax.fori_loop(0, heads, finish, 0)


def per_device(n_sec, n_ctx, doc_lengths, queries, key_states, value_states):
    tokens = queries.shape[0]
    heads = key_states.shape[1] // HEAD
    span = MOST + BLOCK
    rows = 8 * tokens - (6 * tokens - MOST)
    dma = pltpu.SemaphoreType.DMA
    flops = 4 * tokens * span * heads * GROUP * HEAD
    return pl.pallas_call(
        functools.partial(kernel, n_sec, n_ctx),
        out_shape=jax.ShapeDtypeStruct((tokens // n_sec, Q_HEADS * HEAD), jnp.bfloat16),
        in_specs=[pl.BlockSpec(memory_space=pltpu.SMEM)]
        + [pl.BlockSpec(memory_space=pl.ANY)] * 3,
        out_specs=pl.BlockSpec(memory_space=pl.ANY),
        scratch_shapes=[
            pltpu.VMEM((heads, rows, 2 * HEAD), jnp.bfloat16),
            pltpu.VMEM(queries.shape, jnp.bfloat16),
            pltpu.VMEM((heads, tokens, GROUP * HEAD), jnp.bfloat16),
            pltpu.VMEM((tokens // BLOCK, BLOCK, span), jnp.float32),
            dma((2, heads)),
            dma,
            dma((7, heads)),
            dma((7, heads)),
            dma((heads, n_sec)),
            dma((heads, n_sec)),
            dma((heads,)),
        ],
        compiler_params=pltpu.CompilerParams(
            collective_id=0, has_side_effects=True, vmem_limit_bytes=48 * 1024 * 1024),
        cost_estimate=pl.CostEstimate(
            flops=flops, bytes_accessed=5 * 1024 * 1024,
            transcendentals=tokens * span * heads * GROUP),
    )(doc_lengths, queries, key_states, value_states)


def solution(mesh):
    return jax.shard_map(
        functools.partial(per_device, mesh.shape["section"], mesh.shape["ctx"]),
        mesh=mesh,
        in_specs=(P(), P("ctx", "section"), P("ctx", "section"), P("ctx", "section")),
        out_specs=P(("ctx", "section"), None),
        check_vma=False,
    )
```

profile of v0, /device:TPU:8, one launch (start us, length us, event | category | flops | bytes accessed | tf_op | source)
XLA Modules:
  0.0 54.1 jit_solution(9503013595413803372)
XLA Ops:
  0.0 0.0 copy-start
  0.0 1.6 %copy-done = bf16[256,4096]{1,0:T(8,128)(2,1)S(1)} copy-done((bf16[256,4096]{1,0:T(8,128)(2,1)S(1)}, bf16[256,4096]{1,0:T(8,128)(2,1)}, u32[]{:S(2)}) %copy-start) | copy-done | bytes 2097176
  1.6 0.0 copy-start.1
  1.6 0.9 %copy-done.1 = bf16[256,512]{1,0:T(8,128)(2,1)S(1)} copy-done((bf16[256,512]{1,0:T(8,128)(2,1)S(1)}, bf16[256,512]{1,0:T(8,128)(2,1)}, u32[]{:S(2)}) %copy-start.1) | copy-done | bytes 262168
  2.5 0.0 copy-start.2
  2.5 0.9 %copy-done.2 = bf16[256,512]{1,0:T(8,128)(2,1)S(1)} copy-done((bf16[256,512]{1,0:T(8,128)(2,1)S(1)}, bf16[256,512]{1,0:T(8,128)(2,1)}, u32[]{:S(2)}) %copy-start.2) | copy-done | bytes 262168
  3.5 0.0 copy-start.3
  3.5 0.7 %copy-done.3 = s32[7]{0:T(128)S(1)} copy-done((s32[7]{0:T(128)S(1)}, s32[7]{0:T(128)}, u32[]{:S(2)}) %copy-start.3) | copy-done | bytes 52
  4.1 48.6 %shard_map.46 = bf16[128,8192]{1,0:T(8,128)(2,1)S(1)} custom-call(s32[7]{0:T(128)S(1)} %copy-done.3, bf16[256,4096]{1,0:T(8,128)(2,1)S(1)} %copy-done, bf16[256,512]{1,0:T(8,128)(2,1)S(1)} %copy-done.1, bf16[256,512]{1,0:T(8,128)(2,1)S(1)} %copy-done.2), custom_call_target="tpu_custom_call" | custom-call | flops 5368709120 | bytes 5242880 | tf_op jit(solution)/shard_map/pallas_call | solution.py:257
  52.8 1.3 %copy.6 = bf16[128,8192]{1,0:T(8,128)(2,1)} copy(bf16[128,8192]{1,0:T(8,128)(2,1)S(1)} %shard_map.46) | data formatting | bytes 4194304
Async XLA Ops:
  0.0 1.6 %copy-start = (bf16[256,4096]{1,0:T(8,128)(2,1)S(1)}, bf16[256,4096]{1,0:T(8,128)(2,1)}, u32[]{:S(2)}) copy-start(bf16[256,4096]{1,0:T(8,128)(2,1)} %q_ref.1) | copy-start | bytes 6291460
  1.6 0.9 %copy-start.1 = (bf16[256,512]{1,0:T(8,128)(2,1)S(1)}, bf16[256,512]{1,0:T(8,128)(2,1)}, u32[]{:S(2)}) copy-start(bf16[256,512]{1,0:T(8,128)(2,1)} %k_ref.1) | copy-start | bytes 786436
  2.5 0.9 %copy-start.2 = (bf16[256,512]{1,0:T(8,128)(2,1)S(1)}, bf16[256,512]{1,0:T(8,128)(2,1)}, u32[]{:S(2)}) copy-start(bf16[256,512]{1,0:T(8,128)(2,1)} %v_ref.1) | copy-start | bytes 786436
  3.5 0.7 %copy-start.3 = (s32[7]{0:T(128)S(1)}, s32[7]{0:T(128)}, u32[]{:S(2)}) copy-start(s32[7]{0:T(128)} %docs_ref.1) | copy-start | bytes 88
where the time goes:
time: 54.3 us; the launch traced here: 54.1 us
  Pallas kernels  48.6 us (90%)
  local copies, waits for them, and re-layouts  5.47 us (10%)
    pallas_call x1, Pallas kernels, per_device(): pl.pallas_call(functools.partial(kernel, n_sec, n_ctx), out_shape=jax.Sha...  48.6 us
    unnamed x9, local copies, waits for them, and re-layouts  5.47 us

commit v1 on v0

--- a/solution.py
+++ b/solution.py
@@ -15,13 +15,18 @@
 GROUP = Q_HEADS // KV_HEADS
 BLOCK = 128
 MESH = pl.DeviceIdType.MESH
+RELAY_AFTER = {(0, 1, 1): 2, (0, 2, 0): 1, (0, 2, 1): 1, (1, 1, 1): 2, (1, 2, 1): 1, (2, 1, 1): 1}
 SCALE = math.log2(math.e) / math.sqrt(HEAD)
+HALVES = 2
+PART = GROUP // HALVES
 UP, SIDE, SIB_A, SIB_B, SIB_C, HALF_Y, HALF_Z = range(7)
 
 
-def kernel(n_sec, n_ctx, docs_ref, q_ref, k_ref, v_ref, out_ref, kv, q, obuf, bias,
-           in_sem, q_sem, send_sem, recv_sem, osend_sem, orecv_sem, own_sem):
-    heads = kv.shape[0]
+def kernel(n_sec, n_ctx, docs_ref, q_ref, k_ref, v_ref, out_ref, kv, q, qx, obuf, bias,
+           in_sem, q_sem, send_sem, recv_sem, osend_sem, orecv_sem, own_sem, x_send, x_recv):
+    heads = k_ref.shape[1] // HEAD
+    extra = kv.shape[0] - heads
+    kvs = kv.shape[0]
     tokens = q.shape[0]
     span = MOST + BLOCK
     rows_out = tokens // n_sec
@@ -115,15 +120,37 @@
                 for condition, _ in greets)
     pl.semaphore_wait(barrier, peers)
 
-    for h in range(heads):
-        load(h, 0).wait()
-        load(h, 1).wait()
+    def spread(h):
         when(has_up, lambda: send(UP, h).start())
         when(y == 0, lambda: send(SIDE, h).start())
         when(j == 0, lambda: send(SIB_A, h).start())
 
+    def cross_kv():
+        return pltpu.make_async_remote_copy(
+            src_ref=kv.at[heads - 1, rows(6 + j)], dst_ref=kv.at[heads, rows(6 + j)],
+            send_sem=x_send.at[0], recv_sem=x_recv.at[0],
+            device_id={"section": 1 - sec}, device_id_type=MESH)
+
+    def cross_q():
+        theirs = pl.ds(pl.multiple_of((1 - sec) * BLOCK, BLOCK), BLOCK)
+        return pltpu.make_async_remote_copy(
+            src_ref=q_ref.at[theirs, pl.ds((heads - 1) * width, width)], dst_ref=qx,
+            send_sem=x_send.at[1], recv_sem=x_recv.at[1],
+            device_id={"section": 1 - sec}, device_id_type=MESH)
+
+    for h in [heads - 1] * extra + list(range(heads - extra)):
+        load(h, 0).wait()
+        load(h, 1).wait()
+        if extra and h == heads - 1:
+            cross_kv().start()
+            cross_q().start()
+        else:
+            spread(h)
+    if extra:
+        spread(heads - 1)
+
     def clear(first, count):
-        kv[:, first:first + count, :] = jnp.zeros((heads, count, 2 * HEAD), kv.dtype)
+        kv[:, first:first + count, :] = jnp.zeros((kvs, count, 2 * HEAD), kv.dtype)
 
     when(z == 0, lambda: clear(2 * tokens - low, 2 * tokens))
     when(pair == 0, lambda: clear(4 * tokens - low, 2 * tokens))
@@ -140,7 +167,7 @@
         key = first - MOST + lax.broadcasted_iota(jnp.int32, (BLOCK, span), 1)
         bias[b] = jnp.where((key >= start) & (key <= pos), 0.0, -1e30)
 
-    def forward(h):
+    def forward_up(h):
         @pl.when(has_down)
         def _():
             wait_recv(UP, h)
@@ -148,11 +175,16 @@
             send(SIB_B, h).start()
             when(is_giver, lambda: send(HALF_Y, h).start())
 
+    def forward_side(h):
         @pl.when(has_c)
         def _():
             wait_recv(SIDE, h)
             send(SIB_C, h).start()
             when(is_giver & has_up, lambda: send(HALF_Z, h).start())
+
+    def spread_cross():
+        cross_kv().wait_recv()
+        spread(heads)
 
     def arrive(h):
         when(j == 1, lambda: wait_recv(SIB_A, h))
@@ -161,75 +193,105 @@
         when((y == 1) & (j == 0) & has_down, lambda: wait_recv(HALF_Y, h))
         when((y == 0) & (j == 0) & (z > 1), lambda: wait_recv(HALF_Z, h))
 
-    def out_columns(source, h):
-        return pl.ds(pl.multiple_of((source * heads + h) * width, width), width)
-
-    def give(h, dest):
-        piece = pl.ds(pl.multiple_of(dest * rows_out, rows_out), rows_out)
-        return pltpu.make_async_remote_copy(
-            src_ref=obuf.at[h, piece], dst_ref=out_ref.at[:, out_columns(sec, h)],
-            send_sem=osend_sem.at[h, dest], recv_sem=orecv_sem.at[h, sec],
+    def out_columns(source, h, p):
+        first = (source * heads + h) * width + p * PART * HEAD
+        return pl.ds(pl.multiple_of(first, PART * HEAD), PART * HEAD)
+
+    def columns(p):
+        return pl.ds(p * PART * HEAD, PART * HEAD)
+
+    def piece(dest):
+        return pl.ds(pl.multiple_of(dest * rows_out, rows_out), rows_out)
+
+    def give(h, p, dest):
+        return pltpu.make_async_remote_copy(
+            src_ref=obuf.at[h, piece(dest), columns(p)],
+            dst_ref=out_ref.at[:, out_columns(sec, h, p)],
+            send_sem=osend_sem.at[h, p, dest], recv_sem=orecv_sem.at[h, p, sec],
             device_id={"section": dest}, device_id_type=MESH)
 
-    def take(h, source):
-        piece = pl.ds(pl.multiple_of(source * rows_out, rows_out), rows_out)
-        return pltpu.make_async_remote_copy(
-            src_ref=obuf.at[h, piece], dst_ref=out_ref.at[:, out_columns(source, h)],
-            send_sem=osend_sem.at[h, source], recv_sem=orecv_sem.at[h, source],
+    def take(h, p, source):
+        return pltpu.make_async_remote_copy(
+            src_ref=obuf.at[h, piece(source), columns(p)],
+            dst_ref=out_ref.at[:, out_columns(source, h, p)],
+            send_sem=osend_sem.at[h, p, source], recv_sem=orecv_sem.at[h, p, source],
             device_id={"section": source}, device_id_type=MESH)
 
-    def keep(h):
-        piece = pl.ds(pl.multiple_of(sec * rows_out, rows_out), rows_out)
+    def keep(h, p):
+        at = out_columns(sec, h, p) if h < heads else out_columns(1 - sec, heads - 1, p)
         return pltpu.make_async_copy(
-            obuf.at[h, piece], out_ref.at[:, out_columns(sec, h)], own_sem.at[h])
-
-    def unit(h, b):
+            obuf.at[h, piece(sec), columns(p)], out_ref.at[:, at], own_sem.at[h, p])
+
+    def work(h, b, p):
         window = pl.ds(pl.multiple_of(j * tokens + b * BLOCK, BLOCK), span)
         lines = pl.ds(pl.multiple_of(b * BLOCK, BLOCK), BLOCK)
         keys = kv[h, window, 0:HEAD]
         values = jnp.concatenate(
             [kv[h, window, HEAD:2 * HEAD], jnp.ones((span, HEAD), kv.dtype)], 1)
         mask = bias[b]
-        part = 4
-        for first in range(0, GROUP, part):
-            columns = pl.ds(pl.multiple_of(h * width + first * HEAD, HEAD), part * HEAD)
-            wide = q[lines, columns]
-            rows_q = jnp.concatenate(
-                [wide[:, i * HEAD:(i + 1) * HEAD] for i in range(part)], 0)
-            scores = lax.dot_general(rows_q, keys, (((1,), (1,)), ((), ())),
-                                     preferred_element_type=jnp.float32)
-            scores = (scores.reshape(part, BLOCK, span) + mask[None]).reshape(
-                part * BLOCK, span)
-            top = jnp.max(scores, axis=1, keepdims=True)
-            weights = jnp.exp2((scores - top) * SCALE).astype(jnp.bfloat16)
-            mixed = jnp.dot(weights, values, preferred_element_type=jnp.float32)
-            result = (mixed[:, :HEAD] / mixed[:, HEAD:]).astype(obuf.dtype)
-            for i in range(part):
-                at = (first + i) * HEAD
-                obuf[h, lines, at:at + HEAD] = result[i * BLOCK:(i + 1) * BLOCK]
+        if h < heads:
+            wide = q[lines, h * width + p * PART * HEAD:h * width + (p + 1) * PART * HEAD]
+        else:
+            wide = qx[:, p * PART * HEAD:(p + 1) * PART * HEAD]
+        rows_q = jnp.concatenate([wide[:, i * HEAD:(i + 1) * HEAD] for i in range(PART)], 0)
+        scores = lax.dot_general(rows_q, keys, (((1,), (1,)), ((), ())),
+                                 preferred_element_type=jnp.float32)
+        scores = (scores.reshape(PART, BLOCK, span) + mask[None]).reshape(PART * BLOCK, span)
+        top = jnp.max(scores, axis=1, keepdims=True)
+        weights = jnp.exp2((scores - top) * SCALE).astype(jnp.bfloat16)
+        mixed = jnp.dot(weights, values, preferred_element_type=jnp.float32)
+        result = (mixed[:, :HEAD] / mixed[:, HEAD:]).astype(obuf.dtype)
+        for i in range(PART):
+            at = (p * PART + i) * HEAD
+            obuf[h, lines, at:at + HEAD] = result[i * BLOCK:(i + 1) * BLOCK]
+
+    def half_unit(h, b, p):
+        work(h, b, p)
+        for i in range(per_block):
+            dest = b * per_block + i
+            when(dest != sec, lambda: give(h, p, dest).start())
+            when(dest == sec, lambda: keep(h, p).start())
 
     blocks = tokens // BLOCK
     my_block = lax.div(sec * rows_out, BLOCK)
-    forward(0)
-    load_q().wait()
-
-    def step(t, carry):
-        h = lax.div(t, blocks)
-        turn = lax.rem(t, blocks)
-        b = lax.rem(my_block + 1 + turn, blocks)
-
-        when(turn == 0, lambda: arrive(h))
-        when((turn == 1) & (h + 1 < heads), lambda: forward(h + 1))
-        unit(h, b)
-        for i in range(per_block):
-            dest = b * per_block + i
-            when(dest != sec, lambda: give(h, dest).start())
-            when(dest == sec, lambda: keep(h).start())
-        return carry
-
-    lax.fori_loop(0, heads * blocks, step, 0)
-
-    def finish(h, carry):
+    units = [(h, turn) for h in range(heads - extra) for turn in range(1, blocks + 1)]
+    units += [(h, blocks) for h in range(heads - extra, kvs)]
+
+    relays = [functools.partial(forward_up, 0)]
+    if extra:
+        relays.append(spread_cross)
+    for h in range(kvs):
+        if h + 1 < kvs:
+            relays.append(functools.partial(forward_up, h + 1))
+        relays.append(functools.partial(forward_side, h))
+    due = {}
+    for h in range(kvs):
+        due[h] = 1 + extra + 2 * (h + 1) - (h + 1 == kvs)
+
+    done = 0
+    reached = -1
+    load_q_waited = False
+    for h, turn in units:
+        if h > reached:
+            while done < due[h]:
+                relays[done]()
+                done += 1
+            if not load_q_waited:
+                load_q().wait()
+                load_q_waited = True
+            arrive(h)
+            if h == heads:
+                cross_q().wait_recv()
+            reached = h
+        b = lax.rem(my_block + turn, blocks)
+        for p in range(HALVES):
+            half_unit(h, b, p)
+            if done < len(relays) and (h, turn, p) in RELAY_AFTER:
+                for _ in range(RELAY_AFTER[h, turn, p]):
+                    relays[done]()
+                    done += 1
+
+    for h in range(kvs):
         when(has_up, lambda: send(UP, h).wait_send())
         when((y == 0) | has_down, lambda: send(SIDE, h).wait_send())
         when(j == 0, lambda: send(SIB_A, h).wait_send())
@@ -237,20 +299,25 @@
         when(has_c, lambda: send(SIB_C, h).wait_send())
         when(is_giver & has_down, lambda: send(HALF_Y, h).wait_send())
         when(is_giver & has_down & has_up, lambda: send(HALF_Z, h).wait_send())
-        keep(h).wait()
-        for offset in range(1, n_sec):
-            other = lax.rem(sec + offset, n_sec)
-            give(h, other).wait_send()
-            take(h, other).wait_recv()
-        return carry
-
-    lax.fori_loop(0, heads, finish, 0)
+        for p in range(HALVES):
+            keep(h, p).wait()
+    if extra:
+        cross_kv().wait_send()
+        cross_q().wait_send()
+    for h in range(heads - extra):
+        for p in range(HALVES):
+            for offset in range(1, n_sec):
+                other = lax.rem(sec + offset, n_sec)
+                give(h, p, other).wait_send()
+                take(h, p, other).wait_recv()
 
 
 def per_device(n_sec, n_ctx, doc_lengths, queries, key_states, value_states):
     tokens = queries.shape[0]
     heads = key_states.shape[1] // HEAD
     span = MOST + BLOCK
+    extra = int(n_sec == 2 and heads > 1)
+    kvs = heads + extra
     rows = 8 * tokens - (6 * tokens - MOST)
     dma = pltpu.SemaphoreType.DMA
     flops = 4 * tokens * span * heads * GROUP * HEAD
@@ -258,23 +325,26 @@
         functools.partial(kernel, n_sec, n_ctx),
         out_shape=jax.ShapeDtypeStruct((tokens // n_sec, Q_HEADS * HEAD), jnp.bfloat16),
         in_specs=[pl.BlockSpec(memory_space=pltpu.SMEM)]
-        + [pl.BlockSpec(memory_space=pl.ANY)] * 3,
+        + [pl.BlockSpec(memory_space=pltpu.HBM)] * 3,
         out_specs=pl.BlockSpec(memory_space=pl.ANY),
         scratch_shapes=[
-            pltpu.VMEM((heads, rows, 2 * HEAD), jnp.bfloat16),
+            pltpu.VMEM((kvs, rows, 2 * HEAD), jnp.bfloat16),
             pltpu.VMEM(queries.shape, jnp.bfloat16),
-            pltpu.VMEM((heads, tokens, GROUP * HEAD), jnp.bfloat16),
+            pltpu.VMEM((BLOCK, GROUP * HEAD), jnp.bfloat16),
+            pltpu.VMEM((kvs, tokens, GROUP * HEAD), jnp.bfloat16),
             pltpu.VMEM((tokens // BLOCK, BLOCK, span), jnp.float32),
             dma((2, heads)),
             dma,
-            dma((7, heads)),
-            dma((7, heads)),
-            dma((heads, n_sec)),
-            dma((heads, n_sec)),
-            dma((heads,)),
+            dma((7, kvs)),
+            dma((7, kvs)),
+            dma((heads, HALVES, n_sec)),
+            dma((heads, HALVES, n_sec)),
+            dma((kvs, HALVES)),
+            dma((2,)),
+            dma((2,)),
         ],
         compiler_params=pltpu.CompilerParams(
-            collective_id=0, has_side_effects=True, vmem_limit_bytes=48 * 1024 * 1024),
+            collective_id=0, has_side_effects=True, vmem_limit_bytes=60 * 1024 * 1024),
         cost_estimate=pl.CostEstimate(
             flops=flops, bytes_accessed=5 * 1024 * 1024,
             transcendentals=tokens * span * heads * GROUP),

time: 54.3 us -> 51.3 us (0.945)
  the two profiles are of different devices: /device:TPU:8 before, /device:TPU:18 now
where the time goes in v1:
time: 51.3 us; the launch traced here: 51.2 us
  Pallas kernels  48.1 us (94%)
  local copies, waits for them, and re-layouts  3.1 us (6%)
    pallas_call x1, Pallas kernels, per_device(): pl.pallas_call(functools.partial(kernel, n_sec, n_ctx), out_shape=jax.Sha...  48.1 us
    unnamed x1, local copies, waits for them, and re-layouts  3.1 us

profile of v1, /device:TPU:18, one launch (start us, length us, event | category | flops | bytes accessed | tf_op | source)
XLA Modules:
  0.0 51.2 jit_solution(12571864206342194765)
XLA Ops:
  0.0 48.1 %shard_map.46 = bf16[128,8192]{1,0:T(8,128)(2,1)} custom-call(s32[7]{0:T(128)} %docs_ref.1, bf16[256,4096]{1,0:T(8,128)(2,1)} %q_ref.1, bf16[256,512]{1,0:T(8,128)(2,1)} %k_ref.1, bf16[256,512]{1,0:T(8,128)(2,1)} %v_ref.1), custom_call_target="tpu_custom_call" | custom-call | flops 5368709120 | bytes 5242880 | tf_op jit(solution)/shard_map/pallas_call | solution.py:324
  48.1 3.1 %copy.6 = bf16[128,8192]{1,0:T(8,128)(2,1)} copy(bf16[128,8192]{1,0:T(8,128)(2,1)} %shard_map.46) | data formatting | bytes 4194304
